TPU v7x, 768 devices: a whole 4x8x12 slice. The times are simulated.
768 devices in a mesh: row: 8 (over y), inner: 6 (over z_lo), out: 16 (over z_hi, x, core).
Axes of the slice: x: 4, y: 8, z: 12 (z_hi: 2, z_lo: 6; z = z_hi * 6 + z_lo), core: 2. Of those that a mesh axis runs over, the one named last changes fastest.
Arguments:
- tokens: bfloat16 [384, 8192], P(('inner', 'out'), 'row'), may hold values from -6 to 6
- grad_out: bfloat16 [384, 8192], P(('inner', 'out'), 'row'), may hold values from -6 to 6
- gate_weight: bfloat16 [8192, 24576], P('row', ('inner', 'out')), may hold values from -0.0625 to 0.0625
- up_weight: bfloat16 [8192, 24576], P('row', ('inner', 'out')), may hold values from -0.0625 to 0.0625
- down_weight: bfloat16 [24576, 8192], P(('inner', 'out'), 'row'), may hold values from -0.0390625 to 0.0390625
Outputs:
- mixed: bfloat16 [384, 8192], P(('inner', 'out'), 'row')
- grad_tokens: bfloat16 [384, 8192], P(('inner', 'out'), 'row')
- grad_gate: bfloat16 [8192, 24576], P('row', ('inner', 'out'))
- grad_up: bfloat16 [8192, 24576], P('row', ('inner', 'out'))
- grad_down: bfloat16 [24576, 8192], P(('inner', 'out'), 'row')
All inputs are finite; a program needn't handle non-finite values.
Results may differ from a plain program's by a relative error of at most 0.005.
Values may be sent and summed in bfloat16 or wider, within the bound.
A program may use at most 32 MiB of HBM per device.

v0:
```python
import jax
import jax.numpy as jnp
from jax import lax
from jax.sharding import PartitionSpec as P


def contract_cols(left, right):
    return lax.dot_general(
        left, right, (((1,), (1,)), ((), ())), preferred_element_type=jnp.float32
    )


def contract_rows(left, right):
    return lax.dot_general(
        left, right, (((0,), (0,)), ((), ())), preferred_element_type=jnp.float32
    )


def pointwise(gate, up, back):
    sig = jax.nn.sigmoid(gate)
    hidden = (gate * sig * up).astype(jnp.bfloat16)
    d_up = (back * gate * sig).astype(jnp.bfloat16)
    d_gate = (back * up * sig * (1.0 + gate * (1.0 - sig))).astype(jnp.bfloat16)
    return (hidden, d_gate, d_up)


def on_device(tokens, grad_out, gate_weight, up_weight, down_weight):
    tok_all, grad_all = (
        lax.all_gather(tokens, ("inner", "out"), axis=0, tiled=True),
        lax.all_gather(grad_out, ("inner", "out"), axis=0, tiled=True),
    )
    gate_term = jnp.dot(tok_all, gate_weight, preferred_element_type=jnp.float32)
    up_term = jnp.dot(tok_all, up_weight, preferred_element_type=jnp.float32)
    back_term = contract_cols(grad_all, down_weight)
    gate, up, back = (
        lax.psum_scatter(gate_term, "row", scatter_dimension=0, tiled=True),
        lax.psum_scatter(up_term, "row", scatter_dimension=0, tiled=True),
        lax.psum_scatter(back_term, "row", scatter_dimension=0, tiled=True),
    )
    hidden, d_gate, d_up = pointwise(gate, up, back)
    hidden, d_gate, d_up = (
        lax.all_gather(hidden, "row", axis=0, tiled=True),
        lax.all_gather(d_gate, "row", axis=0, tiled=True),
        lax.all_gather(d_up, "row", axis=0, tiled=True),
    )
    mixed_term = jnp.dot(hidden, down_weight, preferred_element_type=jnp.float32)
    input_term = contract_cols(d_gate, gate_weight) + contract_cols(d_up, up_weight)
    mixed, grad_tokens = (
        lax.psum_scatter(mixed_term, ("inner", "out"), scatter_dimension=0, tiled=True),
        lax.psum_scatter(input_term, ("inner", "out"), scatter_dimension=0, tiled=True),
    )
    grad_gate = contract_rows(tok_all, d_gate).astype(jnp.bfloat16)
    grad_up = contract_rows(tok_all, d_up).astype(jnp.bfloat16)
    grad_down = contract_rows(hidden, grad_all).astype(jnp.bfloat16)
    return (
        mixed.astype(jnp.bfloat16),
        grad_tokens.astype(jnp.bfloat16),
        grad_gate,
        grad_up,
        grad_down,
    )


def solution(mesh):
    in_specs = (
        P(("inner", "out"), "row"),
        P(("inner", "out"), "row"),
        P("row", ("inner", "out")),
        P("row", ("inner", "out")),
        P(("inner", "out"), "row"),
    )
    out_specs = (
        P(("inner", "out"), "row"),
        P(("inner", "out"), "row"),
        P("row", ("inner", "out")),
        P("row", ("inner", "out")),
        P(("inner", "out"), "row"),
    )
    return jax.shard_map(
        on_device, mesh=mesh, in_specs=in_specs, out_specs=out_specs, check_vma=False
    )
```

profile of v0, /device:TPU:79, one launch (start us, length us, event | category | flops | bytes accessed | tf_op | source)
XLA Modules:
  0.0 1138.6 jit_solution(682488018000155663)
XLA Ops:
  7.2 0.0 copy-start
  7.2 0.0 copy-start.3
  7.2 0.0 reduce-scatter.6.cloned.1.call-start
  7.2 170.7 %all-gather = bf16[96,4,1024]{2,1,0:T(4,128)(2,1)S(1)} all-gather(bf16[1,4,1024]{2,1,0:T(4,128)(2,1)} %bitcast.25), channel_id=1, replica_groups=mesh['row'=8,'inner'=6,'out'=16] {'inner','out'}, dimensions={0}, use_global_device_ids=true | all-gather | bytes 794624 | tf_op jit(solution)/shard_map/all_gather | solution.py:29
  177.9 0.2 reshape.11
  178.1 0.0 copy-done.3
  178.1 1.1 fusion.3
  179.3 0.0 copy-start.7
  179.3 0.0 reduce-scatter.6.cloned.1.call-update
  179.3 0.0 reduce-scatter.4.cloned.1.call-start
  179.3 0.0 copy-done
  179.3 1.1 fusion.2
  180.5 0.0 copy-start.1
  180.5 0.0 reduce-scatter.4.cloned.1.call-update
  180.5 0.0 reduce-scatter.8.cloned.1.call-start
  180.5 0.0 copy-done.7
  180.6 167.9 %all-gather.1 = bf16[96,4,1024]{2,1,0:T(4,128)(2,1)S(1)} all-gather(bf16[1,4,1024]{2,1,0:T(4,128)(2,1)S(1)} %bitcast.26), channel_id=1, replica_groups=mesh['row'=8,'inner'=6,'out'=16] {'inner','out'}, dimensions={0}, use_global_device_ids=true | all-gather | bytes 794624 | tf_op jit(solution)/shard_map/all_gather | solution.py:30
  348.5 0.2 reshape.13
  348.6 0.0 copy-done.1
  348.6 1.2 fusion.5
  349.8 0.0 reduce-scatter.8.cloned.1.call-update
  349.8 1.3 dynamic-slice
  351.8 0.0 reduce-scatter.6.cloned.1.call-done
  351.8 0.0 reduce-scatter.4.cloned.1.call-done
  351.8 36.1 %reduce-scatter.8.cloned.1.call-done = f32[48,256]{1,0:T(8,128)} async-done(((f32[384,256]{1,0:T(8,128)}), f32[48,256]{1,0:T(8,128)}) %reduce-scatter.8.cloned.1.call-update) | async-done | bytes 49168 | tf_op jit(solution)/shard_map/reduce_scatter | solution.py:38
  387.9 0.9 multiply_convert_fusion
  388.8 18.5 %all_gather.18 = bf16[384,256]{1,0:T(8,128)(2,1)S(1)} all-gather(bf16[48,256]{1,0:T(8,128)(2,1)S(1)} %get-tuple-element.18), channel_id=1, replica_groups=mesh['row'=8,'inner'=6,'out'=16] {'row'}, dimensions={0}, use_global_device_ids=true | all-gather | bytes 221184 | tf_op jit(solution)/shard_map/all_gather | solution.py:43
  407.3 0.5 fusion
  407.7 0.0 copy-start.2
  407.7 1.6 fusion.6
  409.3 19.0 %all_gather.16 = bf16[384,256]{1,0:T(8,128)(2,1)S(1)} all-gather(bf16[48,256]{1,0:T(8,128)(2,1)S(1)} %get-tuple-element.19), channel_id=1, replica_groups=mesh['row'=8,'inner'=6,'out'=16] {'row'}, dimensions={0}, use_global_device_ids=true | all-gather | bytes 221184 | tf_op jit(solution)/shard_map/all_gather | solution.py:42
  428.3 1.3 convolution_convert_fusion
  429.5 0.0 copy-done.2
  429.5 0.4 fusion.4
  429.9 18.5 %all_gather.19 = bf16[384,256]{1,0:T(8,128)(2,1)S(1)} all-gather(bf16[48,256]{1,0:T(8,128)(2,1)S(1)} %get-tuple-element.17), channel_id=1, replica_groups=mesh['row'=8,'inner'=6,'out'=16] {'row'}, dimensions={0}, use_global_device_ids=true | all-gather | bytes 221184 | tf_op jit(solution)/shard_map/all_gather | solution.py:44
  448.4 0.0 copy-start.5
  448.4 0.7 copy-done.5
  449.1 1.3 fusion.1
  450.4 0.0 copy-start.4
  450.4 0.0 copy-start.6
  450.4 2.1 copy.13
  452.5 1.0 copy.12
  453.5 0.0 copy-done.4
  453.5 0.0 copy-done.6
  453.5 3.0 convolution_add_fusion
  456.4 674.3 %all-reduce.4 = (bf16[384,1024]{1,0:T(8,128)(2,1)S(1)}, bf16[384,1024]{1,0:T(8,128)(2,1)}) all-reduce(f32[384,1024]{1,0:T(8,128)S(1)} %fusion.4, f32[384,1024]{1,0:T(8,128)} %convolution_add_fusion), channel_id=4, replica_groups=mesh['row'=8,'inner'=6,'out'=16] {'inner','out'}, use_global_device_ids=true, to_apply=%region_2.0.clone | all-reduce | flops 786432 | bytes 4718592
  1130.8 1.3 dynamic-slice_convert_fusion
Async XLA Ops:
  7.2 172.2 %copy-start = (bf16[1024,256]{1,0:T(8,128)(2,1)S(1)}, bf16[1024,256]{1,0:T(8,128)(2,1)}, u32[]{:S(2)}) copy-start(bf16[1024,256]{1,0:T(8,128)(2,1)} %param.7) | copy-start | bytes 1572868
  7.2 171.0 %copy-start.3 = (bf16[1024,256]{1,0:T(8,128)(2,1)S(1)}, bf16[1024,256]{1,0:T(8,128)(2,1)}, u32[]{:S(2)}) copy-start(bf16[1024,256]{1,0:T(8,128)(2,1)} %param.8) | copy-start | bytes 1572868
  7.2 344.6 %reduce-scatter.6.cloned.1.call-start = ((), (), s32[]{:S(2)}) async-start(), calls=%async_computation.4 | async-start | bytes 442368 | tf_op jit(solution)/shard_map/reduce_scatter | solution.py:37
  179.3 1.3 copy-start.7
  179.3 172.5 %reduce-scatter.4.cloned.1.call-start = ((), (), s32[]{:S(2)}) async-start(), calls=%async_computation.3 | async-start | bytes 442368 | tf_op jit(solution)/shard_map/reduce_scatter | solution.py:36
  180.5 168.2 %copy-start.1 = (bf16[256,1024]{1,0:T(8,128)(2,1)S(1)}, bf16[256,1024]{1,0:T(8,128)(2,1)}, u32[]{:S(2)}) copy-start(bf16[256,1024]{1,0:T(8,128)(2,1)} %param.9) | copy-start | bytes 1572868
  180.5 207.4 %reduce-scatter.8.cloned.1.call-start = ((), (), s32[]{:S(2)}) async-start(), calls=%async_computation.5 | async-start | bytes 442368 | tf_op jit(solution)/shard_map/reduce_scatter | solution.py:38
  407.7 21.8 %copy-start.2 = (bf16[256,1024]{1,0:T(8,128)(2,1)S(1)}, bf16[256,1024]{1,0:T(8,128)(2,1)}, u32[]{:S(2)}) copy-start(bf16[256,1024]{1,0:T(8,128)(2,1)} %param.9) | copy-start | bytes 1572868
  448.4 0.7 copy-start.5
  450.4 3.1 copy-start.4
  450.4 3.1 copy-start.6
Sparse Core Ops, SparseCore 0:
  179.4 38.3 reduce-scatter.5
  221.8 41.2 reduce-scatter.3
  349.9 37.8 reduce-scatter.7
where the time goes:
time: 1140 us
  blocking collectives  1070 us (94%)
  waiting for transfers between devices  36.2 us (3%)
  between operations  14.5 us (1%)
    unnamed x1, blocking collectives  674 us
    all_gather x1, blocking collectives, on_device(): lax.all_gather(tokens, ('inner', 'out'), axis=0, tiled=True)  171 us
    all_gather x1, blocking collectives, on_device(): lax.all_gather(grad_out, ('inner', 'out'), axis=0, tiled=True)  168 us
    reduce_scatter x1, waiting for transfers between devices, on_device(): lax.psum_scatter(back_term, 'row', scatter_dimension=0, tiled=True)  36.1 us
  transfers between devices with their start and end apart: 3, of which 1 were waited for; matrix products, arithmetic and copies ran while one was open for 0% of the time, Pallas kernels for 0%

commit v1 on v0

v1 whole, which is shorter than its diff:
```python
import functools

import jax
import jax.numpy as jnp
from jax import lax
from jax.experimental import pallas as pl
from jax.experimental.pallas import tpu as pltpu
from jax.sharding import PartitionSpec as P

MESH = pl.DeviceIdType.MESH
BF16, F32 = jnp.bfloat16, jnp.float32

NX, NY, NZ = 4, 8, 12
Z_LO = 6
TB = 4
D = 1024
F = 256
CT = NZ * TB
ROWS, LANES = CT // 2, 128
ORDER = (0, 1, 3, 2)


def dot(a, b):
    return jnp.dot(a, b, preferred_element_type=F32)


def dot_nt(a, b):
    return lax.dot_general(a, b, (((1,), (1,)), ((), ())), preferred_element_type=F32)


def dot_tn(a, b):
    return lax.dot_general(a, b, (((0,), (0,)), ((), ())), preferred_element_type=F32)


def kernel(
    tok, gout, wg_in, wu_in, wd_in,
    mixed, gtok, ggate, gup, gdown,
    X, Wg, Wu, Wd, T, G, S1, R1, R2, H, HP, SX, RX, OX, SZ, RZ, A1, A2, A3,
    w_sem, wx_send, wx_recv, z_send, z_recv, x_send, x_recv, t_send, t_recv,
    y1_send, y1_recv, y2_send, y2_recv, h_send, h_recv,
    rx_send, rx_recv, rz_send, rz_recv, o_sem,
):
    y = lax.axis_index("row")
    z = lax.axis_index("inner")
    o = lax.axis_index("out")
    core = lax.rem(o, 2)
    x = lax.rem(o // 2, NX)
    z = z + Z_LO * (o // (2 * NX))

    def at(dx=0, dy=0, dz=0, dc=0):
        xx = lax.rem(x + dx, NX)
        zz = lax.rem(z + dz, NZ)
        cc = lax.rem(core + dc, 2)
        return (
            lax.rem(y + dy, NY),
            lax.rem(zz, Z_LO),
            ((zz // Z_LO) * NX + xx) * 2 + cc,
        )

    def send(src, dst, ssem, rsem, to):
        copy = pltpu.make_async_remote_copy(
            src_ref=src, dst_ref=dst, send_sem=ssem, recv_sem=rsem,
            device_id=to, device_id_type=MESH,
        )
        copy.start()

    def wait(ref, sem):
        pltpu.make_async_copy(ref, ref, sem).wait()

    barrier = pltpu.get_barrier_semaphore()
    peers = (
        [at(dz=d) for d in range(1, NZ)]
        + [at(dx=d) for d in range(1, NX)]
        + [at(dy=d) for d in range(1, NY)]
        + [at(dc=1)]
    )
    for peer in peers:
        pl.semaphore_signal(barrier, inc=1, device_id=peer, device_id_type=MESH)

    weights = ((wg_in, Wg), (wu_in, Wu), (wd_in, Wd))
    for i, (src, dst) in enumerate(weights):
        pltpu.make_async_copy(src, dst.at[0], w_sem.at[i]).start()

    X[0, 0] = jnp.concatenate([tok[...].astype(F32), gout[...].astype(F32)], axis=0).astype(BF16)

    pl.semaphore_wait(barrier, len(peers))

    near = [1, 11, 2, 10, 3, 9, 4, 8, 5, 7, 6]

    def to_x(dz):
        for dx in (1, 3, 2):
            send(X.at[0, dz], X.at[NX - dx, dz], x_send, x_recv.at[NX - dx - 1], at(dx=dx))

    for dz in near:
        send(X.at[0, 0], X.at[0, NZ - dz], z_send, z_recv.at[NZ - dz - 1], at(dz=dz))
    to_x(0)
    partner = at(dc=1)
    for i, (src, dst) in enumerate(weights):
        send(src, dst.at[1], wx_send.at[i], wx_recv.at[i], partner)
    for dz in near:
        wait(X.at[0, dz], z_recv.at[dz - 1])
        to_x(dz)

    low = lax.broadcasted_iota(jnp.int32, (NZ // 2, 8, D), 1) < TB

    def front(j):
        if j:
            wait(X.at[j], x_recv.at[j - 1])
        rows = pl.ds(CT * j, CT)
        v = X[j].astype(F32).reshape(NZ // 2, 2, 8, D)
        even, odd = v[:, 0], v[:, 1]
        t = jnp.where(low, even, pltpu.roll(odd, TB, 1)).reshape(CT, D).astype(BF16)
        g = jnp.where(low, pltpu.roll(even, TB, 1), odd).reshape(CT, D).astype(BF16)
        T[0, rows] = t
        G[0, rows] = g
        send(T.at[0, rows], T.at[1, rows], t_send.at[0], t_recv.at[0], partner)
        send(G.at[0, rows], G.at[1, rows], t_send.at[1], t_recv.at[1], partner)
        for h in range(2):
            if j == 0:
                for i, (src, dst) in enumerate(weights):
                    wait(dst.at[h], (wx_recv if h else w_sem).at[i])
            parts = (dot(t, Wg[h]), dot(t, Wu[h]), dot_nt(g, Wd[h]))
            for half in range(2):
                for c in range(2):
                    q = 4 * half + 2 * h + c
                    for a, part in enumerate(parts):
                        S1[j, q, a] = part[ROWS * half : ROWS * (half + 1), LANES * c : LANES * (c + 1)].astype(BF16)
        for d in (4, 3, 5, 2, 6, 1, 7):
            q = lax.rem(y + d, NY)
            send(S1.at[j, q], R1.at[j, NY - d - 1], y1_send.at[j], y1_recv.at[j], at(dy=d))

    def middle(j):
        wait(R1.at[j], y1_recv.at[j])
        gate, up, back = (
            S1[j, y, a].astype(F32) + jnp.sum(R1[j, :, a].astype(F32), axis=0)
            for a in range(3)
        )
        sig = jax.nn.sigmoid(gate)
        R2[j, y, 0] = (gate * sig * up).astype(BF16)
        R2[j, y, 1] = (back * up * sig * (1.0 + gate * (1.0 - sig))).astype(BF16)
        R2[j, y, 2] = (back * gate * sig).astype(BF16)
        for d in (4, 3, 5, 2, 6, 1, 7):
            send(R2.at[j, y], R2.at[j, y], y2_send.at[j], y2_recv.at[j], at(dy=d))

    def back_end(j):
        wait(R2.at[j, pl.ds(0, NY - 1)], y2_recv.at[j])
        rows = pl.ds(CT * j, CT)
        full = []
        for a in range(3):
            v = jnp.concatenate(
                [
                    jnp.concatenate([R2[j, 4 * half + c, a].astype(F32) for c in range(4)], axis=1)
                    for half in range(2)
                ],
                axis=0,
            ).astype(BF16)
            own, other = v[:, :F], v[:, F:]
            H[0, a, rows] = own
            HP[a, rows] = other
            full.append((own, other))
        for a in range(3):
            send(HP.at[a, rows], H.at[1, a, rows], h_send.at[a], h_recv.at[a], partner)
        (h0, h1), (g0, g1), (u0, u1) = full
        m = (dot(h0, Wd[0]) + dot(h1, Wd[1])).reshape(NZ // 2, 8, D)
        n = (dot_nt(g0, Wg[0]) + dot_nt(g1, Wg[1]) + dot_nt(u0, Wu[0]) + dot_nt(u1, Wu[1])).reshape(NZ // 2, 8, D)
        even = jnp.where(low, m, pltpu.roll(n, TB, 1))
        odd = jnp.where(low, pltpu.roll(m, TB, 1), n)
        for p in range(NZ // 2):
            if j:
                SX[j - 1, 2 * p] = even[p].astype(BF16)
                SX[j - 1, 2 * p + 1] = odd[p].astype(BF16)
            else:
                OX[2 * p] = even[p]
                OX[2 * p + 1] = odd[p]
        if j:
            send(SX.at[j - 1], RX.at[NX - j - 1], rx_send.at[j - 1], rx_recv.at[NX - j - 1], at(dx=j))

    stages = []
    for k in range(len(ORDER) + 4):
        if k < 4:
            front(ORDER[k])
        if 0 <= k - 1 < 4:
            middle(ORDER[k - 1])
        if 0 <= k - 2 < 4:
            back_end(ORDER[k - 2])

    for i in range(2):
        wait(T.at[1], t_recv.at[0]) if i == 0 else wait(G.at[1], t_recv.at[1])
    for a in range(3):
        wait(H.at[1, a], h_recv.at[a])
    for a, (buf, out) in enumerate(((A1, ggate), (A2, gup))):
        buf[...] = (dot_tn(T[0], H[0, a + 1]) + dot_tn(T[1], H[1, a + 1])).astype(BF16)
        pltpu.make_async_copy(buf, out, o_sem.at[a]).start()

    for s in range(NX - 1):
        wait(RX.at[s], rx_recv.at[s])
    for dz in near[::-1]:
        SZ[dz - 1] = (OX[dz] + RX[0, dz].astype(F32) + RX[1, dz].astype(F32) + RX[2, dz].astype(F32)).astype(BF16)
        send(SZ.at[dz - 1], RZ.at[NZ - dz - 1], rz_send, rz_recv, at(dz=dz))
    total = OX[0] + RX[0, 0].astype(F32) + RX[1, 0].astype(F32) + RX[2, 0].astype(F32)

    A3[...] = (dot_tn(H[0, 0], G[0]) + dot_tn(H[1, 0], G[1])).astype(BF16)
    pltpu.make_async_copy(A3, gdown, o_sem.at[2]).start()

    wait(RZ, rz_recv)
    total += jnp.sum(RZ[...].astype(F32), axis=0)
    mixed[...] = total[:TB].astype(BF16)
    gtok[...] = total[TB:].astype(BF16)

    wait(RZ, z_send)
    wait(X.at[pl.ds(0, NX - 1)], x_send)
    wait(RZ, rz_send)
    for i, (src, dst) in enumerate(weights):
        wait(dst.at[0], wx_send.at[i])
    wait(T.at[0], t_send.at[0])
    wait(G.at[0], t_send.at[1])
    for a in range(3):
        wait(HP.at[a], h_send.at[a])
        wait(SX.at[a], rx_send.at[a])
    for j in range(NX):
        wait(R1.at[j], y1_send.at[j])
        wait(R1.at[j], y2_send.at[j])
    for a, (buf, out) in enumerate(((A1, ggate), (A2, gup), (A3, gdown))):
        pltpu.make_async_copy(buf, out, o_sem.at[a]).wait()


def on_device(tokens, grad_out, gate_weight, up_weight, down_weight):
    vmem = pl.BlockSpec(memory_space=pltpu.VMEM)
    hbm = pl.BlockSpec(memory_space=pl.ANY)
    dma = pltpu.SemaphoreType.DMA
    return pl.pallas_call(
        kernel,
        name="ffn",
        out_shape=(
            jax.ShapeDtypeStruct((TB, D), BF16),
            jax.ShapeDtypeStruct((TB, D), BF16),
            jax.ShapeDtypeStruct((D, F), BF16),
            jax.ShapeDtypeStruct((D, F), BF16),
            jax.ShapeDtypeStruct((F, D), BF16),
        ),
        in_specs=[vmem, vmem, hbm, hbm, hbm],
        out_specs=(vmem, vmem, hbm, hbm, hbm),
        scratch_shapes=[
            pltpu.VMEM((NX, NZ, 8, D), BF16),
            pltpu.VMEM((2, D, F), BF16),
            pltpu.VMEM((2, D, F), BF16),
            pltpu.VMEM((2, F, D), BF16),
            pltpu.VMEM((2, NX * CT, D), BF16),
            pltpu.VMEM((2, NX * CT, D), BF16),
            pltpu.VMEM((NX, NY, 3, ROWS, LANES), BF16),
            pltpu.VMEM((NX, NY - 1, 3, ROWS, LANES), BF16),
            pltpu.VMEM((NX, NY, 3, ROWS, LANES), BF16),
            pltpu.VMEM((2, 3, NX * CT, F), BF16),
            pltpu.VMEM((3, NX * CT, F), BF16),
            pltpu.VMEM((NX - 1, NZ, 8, D), BF16),
            pltpu.VMEM((NX - 1, NZ, 8, D), BF16),
            pltpu.VMEM((NZ, 8, D), F32),
            pltpu.VMEM((NZ - 1, 8, D), BF16),
            pltpu.VMEM((NZ - 1, 8, D), BF16),
            pltpu.VMEM((D, F), BF16),
            pltpu.VMEM((D, F), BF16),
            pltpu.VMEM((F, D), BF16),
            dma((3,)),
            dma((3,)),
            dma((3,)),
            dma,
            dma((NZ - 1,)),
            dma,
            dma((NX - 1,)),
            dma((2,)),
            dma((2,)),
            dma((NX,)),
            dma((NX,)),
            dma((NX,)),
            dma((NX,)),
            dma((3,)),
            dma((3,)),
            dma((3,)),
            dma((3,)),
            dma,
            dma,
            dma((3,)),
        ],
        compiler_params=pltpu.CompilerParams(
            collective_id=0, has_side_effects=True, vmem_limit_bytes=40 * 2**20
        ),
        cost_estimate=pl.CostEstimate(
            flops=18 * 384 * D * F, bytes_accessed=2**23, transcendentals=2**17
        ),
    )(tokens, grad_out, gate_weight, up_weight, down_weight)


def solution(mesh):
    by_token = P(("inner", "out"), "row")
    by_hidden = P("row", ("inner", "out"))
    return jax.shard_map(
        on_device,
        mesh=mesh,
        in_specs=(by_token, by_token, by_hidden, by_hidden, by_token),
        out_specs=(by_token, by_token, by_hidden, by_hidden, by_token),
        check_vma=False,
    )
```

time: 1140 us -> 81.3 us (0.07)
  the two profiles are of different devices: /device:TPU:79 before, /device:TPU:18 now
where the time goes in v1:
time: 81.3 us; the launch traced here: 81 us
  Pallas kernels  72.2 us (89%)
  local copies, waits for them, and re-layouts  8.09 us (10%)
    pallas_call x1, Pallas kernels, on_device(): pl.pallas_call(kernel, name='ffn', out_shape=(jax.ShapeDtypeStruct((TB, D...  72.2 us
    unnamed x15, local copies, waits for them, and re-layouts  8.09 us

profile of v1, /device:TPU:18, one launch (start us, length us, event | category | flops | bytes accessed | tf_op | source)
XLA Modules:
  0.0 81.0 jit_solution(6894227766527121397)
XLA Ops:
  0.6 0.0 copy-start
  0.6 1.0 %copy-done = bf16[1024,256]{1,0:T(8,128)(2,1)S(1)} copy-done((bf16[1024,256]{1,0:T(8,128)(2,1)S(1)}, bf16[1024,256]{1,0:T(8,128)(2,1)}, u32[]{:S(2)}) %copy-start) | copy-done | bytes 524312
  1.7 0.0 copy-start.1
  1.7 1.0 %copy-done.1 = bf16[1024,256]{1,0:T(8,128)(2,1)S(1)} copy-done((bf16[1024,256]{1,0:T(8,128)(2,1)S(1)}, bf16[1024,256]{1,0:T(8,128)(2,1)}, u32[]{:S(2)}) %copy-start.1) | copy-done | bytes 524312
  2.7 0.0 copy-start.2
  2.7 1.0 %copy-done.2 = bf16[256,1024]{1,0:T(8,128)(2,1)S(1)} copy-done((bf16[256,1024]{1,0:T(8,128)(2,1)S(1)}, bf16[256,1024]{1,0:T(8,128)(2,1)}, u32[]{:S(2)}) %copy-start.2) | copy-done | bytes 524312
  3.8 0.0 copy-start.3
  3.8 0.7 copy-done.3
  4.5 0.0 copy-start.4
  4.5 0.7 copy-done.4
  5.2 72.2 %ffn.1 = (bf16[4,1024]{1,0:T(4,128)(2,1)S(1)}, bf16[4,1024]{1,0:T(4,128)(2,1)S(1)}, bf16[1024,256]{1,0:T(8,128)(2,1)S(1)}, bf16[1024,256]{1,0:T(8,128)(2,1)S(1)}, bf16[256,1024]{1,0:T(8,128)(2,1)S(1)}) custom-call(bf16[4,1024]{1,0:T(4,128)(2,1)S(1)} %copy-done.3, bf16[4,1024]{1,0:T(4,128)(2,1)S(1)} %copy-done.4, bf16[1024,256]{1,0:T(8,128)(2,1)S(1)} %copy-done, ...), custom_call_target="tpu_custom_call" | custom-call | flops 1811939328 | bytes 8388608 | tf_op jit(solution)/shard_map/ffn/pallas_call | solution.py:231
  77.4 0.6 copy.15
  78.0 0.6 copy.16
  78.6 0.8 copy.17
  79.4 0.8 copy.18
  80.2 0.8 copy.19
Async XLA Ops:
  0.6 1.0 %copy-start = (bf16[1024,256]{1,0:T(8,128)(2,1)S(1)}, bf16[1024,256]{1,0:T(8,128)(2,1)}, u32[]{:S(2)}) copy-start(bf16[1024,256]{1,0:T(8,128)(2,1)} %wg_in.1) | copy-start | bytes 1572868
  1.7 1.0 %copy-start.1 = (bf16[1024,256]{1,0:T(8,128)(2,1)S(1)}, bf16[1024,256]{1,0:T(8,128)(2,1)}, u32[]{:S(2)}) copy-start(bf16[1024,256]{1,0:T(8,128)(2,1)} %wu_in.1) | copy-start | bytes 1572868
  2.7 1.0 %copy-start.2 = (bf16[256,1024]{1,0:T(8,128)(2,1)S(1)}, bf16[256,1024]{1,0:T(8,128)(2,1)}, u32[]{:S(2)}) copy-start(bf16[256,1024]{1,0:T(8,128)(2,1)} %wd_in.1) | copy-start | bytes 1572868
  3.8 0.7 copy-start.3
  4.5 0.7 copy-start.4

commit v2 on v1

--- a/solution.py
+++ b/solution.py
@@ -17,6 +17,7 @@
 F = 256
 CT = NZ * TB
 ROWS, LANES = CT // 2, 128
+KNEE4, KNEE2 = 2.0**-12, 2.0**-30
 ORDER = (0, 1, 3, 2)
 
 
@@ -32,11 +33,31 @@
     return lax.dot_general(a, b, (((0,), (0,)), ((), ())), preferred_element_type=F32)
 
 
+def coded4(v):
+    r = jnp.maximum(jnp.abs(v) * (1.0 / KNEE4), 1.0)
+    return (v * (r * r * r)).astype(BF16)
+
+
+def decoded4(c):
+    c = c.astype(F32)
+    root = lax.rsqrt(jnp.maximum(jnp.abs(c) * (1.0 / KNEE4), 1.0))
+    return c * (root * jnp.sqrt(root))
+
+
+def coded2(v):
+    return (v * jnp.maximum(jnp.abs(v) * (1.0 / KNEE2), 1.0)).astype(BF16)
+
+
+def decoded2(c):
+    c = c.astype(F32)
+    return c * lax.rsqrt(jnp.maximum(jnp.abs(c) * (1.0 / KNEE2), 1.0))
+
+
 def kernel(
-    tok, gout, wg_in, wu_in, wd_in,
+    tok_in, gout_in, wg_in, wu_in, wd_in,
     mixed, gtok, ggate, gup, gdown,
-    X, Wg, Wu, Wd, T, G, S1, R1, R2, H, HP, SX, RX, OX, SZ, RZ, A1, A2, A3,
-    w_sem, wx_send, wx_recv, z_send, z_recv, x_send, x_recv, t_send, t_recv,
+    tok, gout, X, Wg, Wu, Wd, T, G, S1, R1, R2, H, HP, SX, RX, OX, SZ, RZ, A1, A2, A3,
+    in_sem, w_sem, wx_send, wx_recv, z_send, z_recv, x_send, x_recv, t_send, t_recv,
     y1_send, y1_recv, y2_send, y2_recv, h_send, h_recv,
     rx_send, rx_recv, rz_send, rz_recv, o_sem,
 ):
@@ -67,6 +88,8 @@
     def wait(ref, sem):
         pltpu.make_async_copy(ref, ref, sem).wait()
 
+    pltpu.make_async_copy(tok_in, tok, in_sem.at[0]).start()
+    pltpu.make_async_copy(gout_in, gout, in_sem.at[1]).start()
     barrier = pltpu.get_barrier_semaphore()
     peers = (
         [at(dz=d) for d in range(1, NZ)]
@@ -81,6 +104,8 @@
     for i, (src, dst) in enumerate(weights):
         pltpu.make_async_copy(src, dst.at[0], w_sem.at[i]).start()
 
+    pltpu.make_async_copy(tok_in, tok, in_sem.at[0]).wait()
+    pltpu.make_async_copy(gout_in, gout, in_sem.at[1]).wait()
     X[0, 0] = jnp.concatenate([tok[...].astype(F32), gout[...].astype(F32)], axis=0).astype(BF16)
 
     pl.semaphore_wait(barrier, len(peers))
@@ -124,7 +149,9 @@
                 for c in range(2):
                     q = 4 * half + 2 * h + c
                     for a, part in enumerate(parts):
-                        S1[j, q, a] = part[ROWS * half : ROWS * (half + 1), LANES * c : LANES * (c + 1)].astype(BF16)
+                        S1[j, q, a] = coded4(
+                            part[ROWS * half : ROWS * (half + 1), LANES * c : LANES * (c + 1)]
+                        )
         for d in (4, 3, 5, 2, 6, 1, 7):
             q = lax.rem(y + d, NY)
             send(S1.at[j, q], R1.at[j, NY - d - 1], y1_send.at[j], y1_recv.at[j], at(dy=d))
@@ -132,7 +159,7 @@
     def middle(j):
         wait(R1.at[j], y1_recv.at[j])
         gate, up, back = (
-            S1[j, y, a].astype(F32) + jnp.sum(R1[j, :, a].astype(F32), axis=0)
+            decoded4(S1[j, y, a]) + jnp.sum(decoded4(R1[j, :, a]), axis=0)
             for a in range(3)
         )
         sig = jax.nn.sigmoid(gate)
@@ -167,8 +194,8 @@
         odd = jnp.where(low, pltpu.roll(m, TB, 1), n)
         for p in range(NZ // 2):
             if j:
-                SX[j - 1, 2 * p] = even[p].astype(BF16)
-                SX[j - 1, 2 * p + 1] = odd[p].astype(BF16)
+                SX[j - 1, 2 * p] = coded2(even[p])
+                SX[j - 1, 2 * p + 1] = coded2(odd[p])
             else:
                 OX[2 * p] = even[p]
                 OX[2 * p + 1] = odd[p]
@@ -195,17 +222,19 @@
     for s in range(NX - 1):
         wait(RX.at[s], rx_recv.at[s])
     for dz in near[::-1]:
-        SZ[dz - 1] = (OX[dz] + RX[0, dz].astype(F32) + RX[1, dz].astype(F32) + RX[2, dz].astype(F32)).astype(BF16)
+        SZ[dz - 1] = coded2(OX[dz] + jnp.sum(decoded2(RX[:, dz]), axis=0))
         send(SZ.at[dz - 1], RZ.at[NZ - dz - 1], rz_send, rz_recv, at(dz=dz))
-    total = OX[0] + RX[0, 0].astype(F32) + RX[1, 0].astype(F32) + RX[2, 0].astype(F32)
+    total = OX[0] + jnp.sum(decoded2(RX[:, 0]), axis=0)
 
     A3[...] = (dot_tn(H[0, 0], G[0]) + dot_tn(H[1, 0], G[1])).astype(BF16)
     pltpu.make_async_copy(A3, gdown, o_sem.at[2]).start()
 
     wait(RZ, rz_recv)
-    total += jnp.sum(RZ[...].astype(F32), axis=0)
-    mixed[...] = total[:TB].astype(BF16)
-    gtok[...] = total[TB:].astype(BF16)
+    total += jnp.sum(decoded2(RZ[...]), axis=0)
+    tok[...] = total[:TB].astype(BF16)
+    gout[...] = total[TB:].astype(BF16)
+    pltpu.make_async_copy(tok, mixed, o_sem.at[3]).start()
+    pltpu.make_async_copy(gout, gtok, o_sem.at[4]).start()
 
     wait(RZ, z_send)
     wait(X.at[pl.ds(0, NX - 1)], x_send)
@@ -220,27 +249,44 @@
     for j in range(NX):
         wait(R1.at[j], y1_send.at[j])
         wait(R1.at[j], y2_send.at[j])
-    for a, (buf, out) in enumerate(((A1, ggate), (A2, gup), (A3, gdown))):
+    for a, (buf, out) in enumerate(((A1, ggate), (A2, gup), (A3, gdown), (tok, mixed), (gout, gtok))):
         pltpu.make_async_copy(buf, out, o_sem.at[a]).wait()
+
+
+PIECES = 4
+
+
+def store(*refs):
+    *pairs, sem = refs
+    n = len(pairs) // 2
+    copies = []
+    for i, (src, dst) in enumerate(zip(pairs[:n], pairs[n:])):
+        rows = src.shape[0] // PIECES if src.shape[0] > TB else TB
+        for k in range(src.shape[0] // rows):
+            part = pl.ds(k * rows, rows)
+            copies.append(pltpu.make_async_copy(src.at[part], dst.at[part], sem.at[i * PIECES + k]))
+    for copy in copies:
+        copy.start()
+    for copy in copies:
+        copy.wait()
 
 
 def on_device(tokens, grad_out, gate_weight, up_weight, down_weight):
     vmem = pl.BlockSpec(memory_space=pltpu.VMEM)
-    hbm = pl.BlockSpec(memory_space=pl.ANY)
+    hbm = pl.BlockSpec(memory_space=pltpu.HBM)
     dma = pltpu.SemaphoreType.DMA
-    return pl.pallas_call(
+    out_shape = tuple(
+        jax.ShapeDtypeStruct(shape, BF16) for shape in ((TB, D), (TB, D), (D, F), (D, F), (F, D))
+    )
+    outs = pl.pallas_call(
         kernel,
         name="ffn",
-        out_shape=(
-            jax.ShapeDtypeStruct((TB, D), BF16),
-            jax.ShapeDtypeStruct((TB, D), BF16),
-            jax.ShapeDtypeStruct((D, F), BF16),
-            jax.ShapeDtypeStruct((D, F), BF16),
-            jax.ShapeDtypeStruct((F, D), BF16),
-        ),
-        in_specs=[vmem, vmem, hbm, hbm, hbm],
-        out_specs=(vmem, vmem, hbm, hbm, hbm),
+        out_shape=out_shape,
+        in_specs=[hbm, hbm, hbm, hbm, hbm],
+        out_specs=(hbm,) * 5,
         scratch_shapes=[
+            pltpu.VMEM((TB, D), BF16),
+            pltpu.VMEM((TB, D), BF16),
             pltpu.VMEM((NX, NZ, 8, D), BF16),
             pltpu.VMEM((2, D, F), BF16),
             pltpu.VMEM((2, D, F), BF16),
@@ -260,6 +306,7 @@
             pltpu.VMEM((D, F), BF16),
             pltpu.VMEM((D, F), BF16),
             pltpu.VMEM((F, D), BF16),
+            dma((2,)),
             dma((3,)),
             dma((3,)),
             dma((3,)),
@@ -279,15 +326,24 @@
             dma((3,)),
             dma,
             dma,
-            dma((3,)),
+            dma((5,)),
         ],
         compiler_params=pltpu.CompilerParams(
-            collective_id=0, has_side_effects=True, vmem_limit_bytes=40 * 2**20
+            collective_id=0, has_side_effects=True, vmem_limit_bytes=62 * 2**20
         ),
         cost_estimate=pl.CostEstimate(
             flops=18 * 384 * D * F, bytes_accessed=2**23, transcendentals=2**17
         ),
     )(tokens, grad_out, gate_weight, up_weight, down_weight)
+    return pl.pallas_call(
+        store,
+        name="store",
+        out_shape=out_shape,
+        in_specs=[hbm] * 5,
+        out_specs=(hbm,) * 5,
+        scratch_shapes=[dma((5 * PIECES,))],
+        compiler_params=pltpu.CompilerParams(vmem_limit_bytes=62 * 2**20),
+    )(*outs)
 
 
 def solution(mesh):

time: 81.3 us -> 123 us (1.51)
  Pallas kernels: 72.2 us -> 122 us
  local copies, waits for them, and re-layouts: 8.09 us -> 0 us
    pallas_call x1 -> x2, Pallas kernels: 72.2 us -> 122 us  [the longest x1 72.9 us: on_device(): pl.pallas_call(kernel, name='ffn', out_shape=out_shape, in_specs=[hbm, hb...]
    unnamed x15 -> x0, local copies, waits for them, and re-layouts: 8.09 us -> none
where the time goes in v2:
time: 123 us
  Pallas kernels  122 us (99%)
    pallas_call x1, Pallas kernels, on_device(): pl.pallas_call(kernel, name='ffn', out_shape=out_shape, in_specs=[hbm, hb...  72.9 us
    pallas_call x1, Pallas kernels, on_device(): pl.pallas_call(store, name='store', out_shape=out_shape, in_specs=[hbm] *...  49.4 us

profile of v2, /device:TPU:18, one launch (start us, length us, event | category | flops | bytes accessed | tf_op | source)
XLA Modules:
  0.0 122.9 jit_solution(3366931330715244960)
XLA Ops:
  0.6 72.9 %ffn.1 = (bf16[4,1024]{1,0:T(4,128)(2,1)}, bf16[4,1024]{1,0:T(4,128)(2,1)}, bf16[1024,256]{1,0:T(8,128)(2,1)}, bf16[1024,256]{1,0:T(8,128)(2,1)}, bf16[256,1024]{1,0:T(8,128)(2,1)}) custom-call(bf16[4,1024]{1,0:T(4,128)(2,1)} %tok_in.1, bf16[4,1024]{1,0:T(4,128)(2,1)} %gout_in.1, bf16[1024,256]{1,0:T(8,128)(2,1)} %wg_in.1, bf16[1024,256]{1,0:T(8,128)(2,1)} %wu_in.1, ...), custom_call_target="tpu_custom_call" | custom-call | flops 1811939328 | bytes 8388608 | tf_op jit(solution)/shard_map/ffn/pallas_call | solution.py:281
  73.5 49.4 %store.1 = (bf16[4,1024]{1,0:T(4,128)(2,1)}, bf16[4,1024]{1,0:T(4,128)(2,1)}, bf16[1024,256]{1,0:T(8,128)(2,1)}, bf16[1024,256]{1,0:T(8,128)(2,1)}, bf16[256,1024]{1,0:T(8,128)(2,1)}) custom-call(bf16[4,1024]{1,0:T(4,128)(2,1)} %get-tuple-element.10.refs_0_, bf16[4,1024]{1,0:T(4,128)(2,1)} %get-tuple-element.11.refs_1_, ...), custom_call_target="tpu_custom_call" | custom-call | tf_op jit(solution)/shard_map/store/pallas_call | solution.py:338

commit v3 on v2

--- a/solution.py
+++ b/solution.py
@@ -18,7 +18,8 @@
 CT = NZ * TB
 ROWS, LANES = CT // 2, 128
 KNEE4, KNEE2 = 2.0**-12, 2.0**-30
-ORDER = (0, 1, 3, 2)
+FRONT = (0, 2, 1, 3)
+BACK = (2, 1, 3, 0)
 
 
 def dot(a, b):
@@ -56,9 +57,9 @@
 def kernel(
     tok_in, gout_in, wg_in, wu_in, wd_in,
     mixed, gtok, ggate, gup, gdown,
-    tok, gout, X, Wg, Wu, Wd, T, G, S1, R1, R2, H, HP, SX, RX, OX, SZ, RZ, A1, A2, A3,
+    tok, gout, X, Wg, Wu, Wd, T, G, S1, K1, S2, R1, R2, H, HP, SX, RX, OX, SZ, RZ, A1, A2, A3,
     in_sem, w_sem, wx_send, wx_recv, z_send, z_recv, x_send, x_recv, t_send, t_recv,
-    y1_send, y1_recv, y2_send, y2_recv, h_send, h_recv,
+    k1_recv, y1_send, y1_recv, y2_send, k2_recv, y2_recv, h_send, h_recv,
     rx_send, rx_recv, rz_send, rz_recv, o_sem,
 ):
     y = lax.axis_index("row")
@@ -94,7 +95,7 @@
     peers = (
         [at(dz=d) for d in range(1, NZ)]
         + [at(dx=d) for d in range(1, NX)]
-        + [at(dy=d) for d in range(1, NY)]
+        + [at(dy=d) for d in (1, 2, NY - 2, NY - 1)]
         + [at(dc=1)]
     )
     for peer in peers:
@@ -113,7 +114,7 @@
     near = [1, 11, 2, 10, 3, 9, 4, 8, 5, 7, 6]
 
     def to_x(dz):
-        for dx in (1, 3, 2):
+        for dx in (2, 1, 3):
             send(X.at[0, dz], X.at[NX - dx, dz], x_send, x_recv.at[NX - dx - 1], at(dx=dx))
 
     for dz in near:
@@ -152,9 +153,27 @@
                         S1[j, q, a] = coded4(
                             part[ROWS * half : ROWS * (half + 1), LANES * c : LANES * (c + 1)]
                         )
-        for d in (4, 3, 5, 2, 6, 1, 7):
-            q = lax.rem(y + d, NY)
-            send(S1.at[j, q], R1.at[j, NY - d - 1], y1_send.at[j], y1_recv.at[j], at(dy=d))
+        via = 2 if j % 2 == 0 else -2
+        for to, q, dst, sem in (
+            (via, 4, K1.at[j, 2], k1_recv),
+            (1, 3, K1.at[j, 0], k1_recv),
+            (-1, -3, K1.at[j, 1], k1_recv),
+            (1, 1, R1.at[j, 0], y1_recv),
+            (-1, -1, R1.at[j, 1], y1_recv),
+        ):
+            send(S1.at[j, around(q)], dst, y1_send.at[j], sem.at[j], at(dy=to % NY))
+
+    def around(d):
+        return lax.rem(y + d % NY, NY)
+
+    def relay(j):
+        wait(K1.at[j], k1_recv.at[j])
+        for i, to in enumerate((2, -2)):
+            v = decoded4(S1[j, around(to)]) + decoded4(K1[j, i])
+            if i == j % 2:
+                v += decoded4(K1[j, 2])
+            S2[j, i] = coded4(v)
+            send(S2.at[j, i], R1.at[j, 2 + i], y1_send.at[j], y1_recv.at[j], at(dy=to % NY))
 
     def middle(j):
         wait(R1.at[j], y1_recv.at[j])
@@ -166,11 +185,18 @@
         R2[j, y, 0] = (gate * sig * up).astype(BF16)
         R2[j, y, 1] = (back * up * sig * (1.0 + gate * (1.0 - sig))).astype(BF16)
         R2[j, y, 2] = (back * gate * sig).astype(BF16)
-        for d in (4, 3, 5, 2, 6, 1, 7):
-            send(R2.at[j, y], R2.at[j, y], y2_send.at[j], y2_recv.at[j], at(dy=d))
+        for to, sem in ((2, k2_recv), (-2, k2_recv), (1, y2_recv), (-1, y2_recv)):
+            send(R2.at[j, y], R2.at[j, y], y2_send.at[j], sem.at[j], at(dy=to % NY))
+
+    def spread(j):
+        wait(R2.at[j, pl.ds(0, 2)], k2_recv.at[j])
+        via = 2 if j % 2 == 0 else -2
+        for to, q in ((via, -via), (1, -2), (-1, 2)):
+            block = R2.at[j, around(q)]
+            send(block, block, y2_send.at[j], y2_recv.at[j], at(dy=to % NY))
 
     def back_end(j):
-        wait(R2.at[j, pl.ds(0, NY - 1)], y2_recv.at[j])
+        wait(R2.at[j, pl.ds(0, NY - 3)], y2_recv.at[j])
         rows = pl.ds(CT * j, CT)
         full = []
         for a in range(3):
@@ -202,14 +228,27 @@
         if j:
             send(SX.at[j - 1], RX.at[NX - j - 1], rx_send.at[j - 1], rx_recv.at[NX - j - 1], at(dx=j))
 
-    stages = []
-    for k in range(len(ORDER) + 4):
-        if k < 4:
-            front(ORDER[k])
-        if 0 <= k - 1 < 4:
-            middle(ORDER[k - 1])
-        if 0 <= k - 2 < 4:
-            back_end(ORDER[k - 2])
+    f, b = FRONT, BACK
+    front(f[0])
+    front(f[1])
+    relay(f[0])
+    front(f[2])
+    relay(f[1])
+    front(f[3])
+    relay(f[2])
+    middle(b[0])
+    relay(f[3])
+    middle(b[1])
+    spread(b[0])
+    middle(b[2])
+    spread(b[1])
+    back_end(b[0])
+    middle(b[3])
+    spread(b[2])
+    back_end(b[1])
+    spread(b[3])
+    back_end(b[2])
+    back_end(b[3])
 
     for i in range(2):
         wait(T.at[1], t_recv.at[0]) if i == 0 else wait(G.at[1], t_recv.at[1])
@@ -247,28 +286,22 @@
         wait(HP.at[a], h_send.at[a])
         wait(SX.at[a], rx_send.at[a])
     for j in range(NX):
-        wait(R1.at[j], y1_send.at[j])
-        wait(R1.at[j], y2_send.at[j])
+        wait(R2.at[j, pl.ds(0, 7)], y1_send.at[j])
+        wait(R2.at[j, pl.ds(0, 7)], y2_send.at[j])
     for a, (buf, out) in enumerate(((A1, ggate), (A2, gup), (A3, gdown), (tok, mixed), (gout, gtok))):
         pltpu.make_async_copy(buf, out, o_sem.at[a]).wait()
 
 
-PIECES = 4
-
-
 def store(*refs):
-    *pairs, sem = refs
-    n = len(pairs) // 2
-    copies = []
-    for i, (src, dst) in enumerate(zip(pairs[:n], pairs[n:])):
-        rows = src.shape[0] // PIECES if src.shape[0] > TB else TB
-        for k in range(src.shape[0] // rows):
-            part = pl.ds(k * rows, rows)
-            copies.append(pltpu.make_async_copy(src.at[part], dst.at[part], sem.at[i * PIECES + k]))
-    for copy in copies:
-        copy.start()
-    for copy in copies:
-        copy.wait()
+    n = (len(refs) - 2) // 3
+    src, dst, held, (read, write) = refs[:n], refs[n : 2 * n], refs[2 * n : 3 * n], refs[3 * n :]
+    for i in range(n):
+        pltpu.make_async_copy(src[i], held[i], read.at[i]).start()
+    for i in range(n):
+        pltpu.make_async_copy(src[i], held[i], read.at[i]).wait()
+        pltpu.make_async_copy(held[i], dst[i], write.at[i]).start()
+    for i in range(n):
+        pltpu.make_async_copy(held[i], dst[i], write.at[i]).wait()
 
 
 def on_device(tokens, grad_out, gate_weight, up_weight, down_weight):
@@ -294,7 +327,9 @@
             pltpu.VMEM((2, NX * CT, D), BF16),
             pltpu.VMEM((2, NX * CT, D), BF16),
             pltpu.VMEM((NX, NY, 3, ROWS, LANES), BF16),
-            pltpu.VMEM((NX, NY - 1, 3, ROWS, LANES), BF16),
+            pltpu.VMEM((NX, 3, 3, ROWS, LANES), BF16),
+            pltpu.VMEM((NX, 2, 3, ROWS, LANES), BF16),
+            pltpu.VMEM((NX, 4, 3, ROWS, LANES), BF16),
             pltpu.VMEM((NX, NY, 3, ROWS, LANES), BF16),
             pltpu.VMEM((2, 3, NX * CT, F), BF16),
             pltpu.VMEM((3, NX * CT, F), BF16),
@@ -316,6 +351,8 @@
             dma((NX - 1,)),
             dma((2,)),
             dma((2,)),
+            dma((NX,)),
+            dma((NX,)),
             dma((NX,)),
             dma((NX,)),
             dma((NX,)),
@@ -341,7 +378,7 @@
         out_shape=out_shape,
         in_specs=[hbm] * 5,
         out_specs=(hbm,) * 5,
-        scratch_shapes=[dma((5 * PIECES,))],
+        scratch_shapes=[pltpu.VMEM(o.shape, o.dtype) for o in out_shape] + [dma((5,)), dma((5,))],
         compiler_params=pltpu.CompilerParams(vmem_limit_bytes=62 * 2**20),
     )(*outs)
 

time: 123 us -> 75.7 us (0.62)
  the two profiles are of different devices: /device:TPU:18 before, /device:TPU:1 now
where the time goes in v3:
time: 75.7 us; the launch traced here: 75.5 us
  Pallas kernels  74.8 us (99%)
    pallas_call x1, Pallas kernels, on_device(): pl.pallas_call(kernel, name='ffn', out_shape=out_shape, in_specs=[hbm, hb...  72.5 us
    pallas_call x1, Pallas kernels, on_device(): pl.pallas_call(store, name='store', out_shape=out_shape, in_specs=[hbm] *...  2.3 us

profile of v3, /device:TPU:1, one launch (start us, length us, event | category | flops | bytes accessed | tf_op | source)
XLA Modules:
  0.0 75.5 jit_solution(11681943271392470234)
XLA Ops:
  0.6 72.5 %ffn.1 = (bf16[4,1024]{1,0:T(4,128)(2,1)}, bf16[4,1024]{1,0:T(4,128)(2,1)}, bf16[1024,256]{1,0:T(8,128)(2,1)}, bf16[1024,256]{1,0:T(8,128)(2,1)}, bf16[256,1024]{1,0:T(8,128)(2,1)}) custom-call(bf16[4,1024]{1,0:T(4,128)(2,1)} %tok_in.1, bf16[4,1024]{1,0:T(4,128)(2,1)} %gout_in.1, bf16[1024,256]{1,0:T(8,128)(2,1)} %wg_in.1, bf16[1024,256]{1,0:T(8,128)(2,1)} %wu_in.1, ...), custom_call_target="tpu_custom_call" | custom-call | flops 1811939328 | bytes 8388608 | tf_op jit(solution)/shard_map/ffn/pallas_call | solution.py:314
  73.2 2.3 %store.1 = (bf16[4,1024]{1,0:T(4,128)(2,1)}, bf16[4,1024]{1,0:T(4,128)(2,1)}, bf16[1024,256]{1,0:T(8,128)(2,1)}, bf16[1024,256]{1,0:T(8,128)(2,1)}, bf16[256,1024]{1,0:T(8,128)(2,1)}) custom-call(bf16[4,1024]{1,0:T(4,128)(2,1)} %get-tuple-element.10.refs_0_, bf16[4,1024]{1,0:T(4,128)(2,1)} %get-tuple-element.11.refs_1_, ...), custom_call_target="tpu_custom_call" | custom-call | tf_op jit(solution)/shard_map/store/pallas_call | solution.py:375

commit v4 on v3

--- a/solution.py
+++ b/solution.py
@@ -18,8 +18,23 @@
 CT = NZ * TB
 ROWS, LANES = CT // 2, 128
 KNEE4, KNEE2 = 2.0**-12, 2.0**-30
-FRONT = (0, 2, 1, 3)
-BACK = (2, 1, 3, 0)
+NC, NG = 4, NZ // 4
+Z_ORDER = (0, 1, 11, 6, 5, 7, 4, 8, 3, 9, 2, 10)
+Z_SENDS = tuple(NZ - dz for dz in Z_ORDER if dz)
+SCHEDULE = (
+    ("pass_on", 0, 1, 2, 3),
+    ("front", 0, 1, 2, 3),
+    ("relay", 0, 1, 2, 3),
+    ("turn", 0),
+    ("middle", 0, 1, 2, 3),
+    ("turn", 1),
+    ("spread", 0, 1, 2, 3),
+    ("back_end", 0, 1, 2, 3),
+    ("finish", 0, 1, 2, 3),
+    ("weight_grad", 0, 1, 2),
+)
+NEAR1 = ()
+NEAR2 = ()
 
 
 def dot(a, b):
@@ -57,7 +72,7 @@
 def kernel(
     tok_in, gout_in, wg_in, wu_in, wd_in,
     mixed, gtok, ggate, gup, gdown,
-    tok, gout, X, Wg, Wu, Wd, T, G, S1, K1, S2, R1, R2, H, HP, SX, RX, OX, SZ, RZ, A1, A2, A3,
+    tok, gout, X, Wg, Wu, Wd, T, G, TT, S1, K1, S2, R1, R2, H, HP, SX, RX, OX, OZ, SZ, RZ, A1, A2, A3,
     in_sem, w_sem, wx_send, wx_recv, z_send, z_recv, x_send, x_recv, t_send, t_recv,
     k1_recv, y1_send, y1_recv, y2_send, k2_recv, y2_recv, h_send, h_recv,
     rx_send, rx_recv, rz_send, rz_recv, o_sem,
@@ -95,7 +110,7 @@
     peers = (
         [at(dz=d) for d in range(1, NZ)]
         + [at(dx=d) for d in range(1, NX)]
-        + [at(dy=d) for d in (1, 2, NY - 2, NY - 1)]
+        + [at(dy=d) for d in (range(1, NY) if NEAR1 or NEAR2 else (1, 2, NY - 2, NY - 1))]
         + [at(dc=1)]
     )
     for peer in peers:
@@ -107,33 +122,34 @@
 
     pltpu.make_async_copy(tok_in, tok, in_sem.at[0]).wait()
     pltpu.make_async_copy(gout_in, gout, in_sem.at[1]).wait()
-    X[0, 0] = jnp.concatenate([tok[...].astype(F32), gout[...].astype(F32)], axis=0).astype(BF16)
+    here = Z_ORDER.index(0)
+    X[here, 0] = jnp.concatenate([tok[...].astype(F32), gout[...].astype(F32)], axis=0).astype(BF16)
 
     pl.semaphore_wait(barrier, len(peers))
 
-    near = [1, 11, 2, 10, 3, 9, 4, 8, 5, 7, 6]
-
-    def to_x(dz):
+    def to_x(p):
         for dx in (2, 1, 3):
-            send(X.at[0, dz], X.at[NX - dx, dz], x_send, x_recv.at[NX - dx - 1], at(dx=dx))
-
-    for dz in near:
-        send(X.at[0, 0], X.at[0, NZ - dz], z_send, z_recv.at[NZ - dz - 1], at(dz=dz))
-    to_x(0)
+            send(X.at[p, 0], X.at[p, NX - dx], x_send, x_recv.at[p // NG], at(dx=dx))
+
+    for dz in Z_SENDS:
+        send(X.at[here, 0], X.at[Z_ORDER.index(NZ - dz), 0], z_send, z_recv.at[NZ - dz - 1], at(dz=dz))
+    to_x(here)
     partner = at(dc=1)
     for i, (src, dst) in enumerate(weights):
         send(src, dst.at[1], wx_send.at[i], wx_recv.at[i], partner)
-    for dz in near:
-        wait(X.at[0, dz], z_recv.at[dz - 1])
-        to_x(dz)
+
+    def pass_on(k):
+        for p in range(NG * k, NG * (k + 1)):
+            if p != here:
+                wait(X.at[p, 0], z_recv.at[Z_ORDER[p] - 1])
+                to_x(p)
 
     low = lax.broadcasted_iota(jnp.int32, (NZ // 2, 8, D), 1) < TB
 
     def front(j):
-        if j:
-            wait(X.at[j], x_recv.at[j - 1])
+        wait(RX.at[0], x_recv.at[j])
         rows = pl.ds(CT * j, CT)
-        v = X[j].astype(F32).reshape(NZ // 2, 2, 8, D)
+        v = X[NG * j : NG * (j + 1)].astype(F32).reshape(NZ // 2, 2, 8, D)
         even, odd = v[:, 0], v[:, 1]
         t = jnp.where(low, even, pltpu.roll(odd, TB, 1)).reshape(CT, D).astype(BF16)
         g = jnp.where(low, pltpu.roll(even, TB, 1), odd).reshape(CT, D).astype(BF16)
@@ -153,6 +169,10 @@
                         S1[j, q, a] = coded4(
                             part[ROWS * half : ROWS * (half + 1), LANES * c : LANES * (c + 1)]
                         )
+        if j in NEAR1:
+            for d in (4, 3, 5, 2, 6, 1, 7):
+                send(S1.at[j, around(d)], R1.at[j, NY - d - 1], y1_send.at[j], y1_recv.at[j], at(dy=d))
+            return
         via = 2 if j % 2 == 0 else -2
         for to, q, dst, sem in (
             (via, 4, K1.at[j, 2], k1_recv),
@@ -167,6 +187,8 @@
         return lax.rem(y + d % NY, NY)
 
     def relay(j):
+        if j in NEAR1:
+            return
         wait(K1.at[j], k1_recv.at[j])
         for i, to in enumerate((2, -2)):
             v = decoded4(S1[j, around(to)]) + decoded4(K1[j, i])
@@ -176,19 +198,26 @@
             send(S2.at[j, i], R1.at[j, 2 + i], y1_send.at[j], y1_recv.at[j], at(dy=to % NY))
 
     def middle(j):
-        wait(R1.at[j], y1_recv.at[j])
+        came = NY - 1 if j in NEAR1 else 4
+        wait(R1.at[j, pl.ds(0, came)], y1_recv.at[j])
         gate, up, back = (
-            decoded4(S1[j, y, a]) + jnp.sum(decoded4(R1[j, :, a]), axis=0)
+            decoded4(S1[j, y, a]) + jnp.sum(decoded4(R1[j, :came, a]), axis=0)
             for a in range(3)
         )
         sig = jax.nn.sigmoid(gate)
         R2[j, y, 0] = (gate * sig * up).astype(BF16)
         R2[j, y, 1] = (back * up * sig * (1.0 + gate * (1.0 - sig))).astype(BF16)
         R2[j, y, 2] = (back * gate * sig).astype(BF16)
+        if j in NEAR2:
+            for d in (4, 3, 5, 2, 6, 1, 7):
+                send(R2.at[j, y], R2.at[j, y], y2_send.at[j], y2_recv.at[j], at(dy=d))
+            return
         for to, sem in ((2, k2_recv), (-2, k2_recv), (1, y2_recv), (-1, y2_recv)):
             send(R2.at[j, y], R2.at[j, y], y2_send.at[j], sem.at[j], at(dy=to % NY))
 
     def spread(j):
+        if j in NEAR2:
+            return
         wait(R2.at[j, pl.ds(0, 2)], k2_recv.at[j])
         via = 2 if j % 2 == 0 else -2
         for to, q in ((via, -via), (1, -2), (-1, 2)):
@@ -196,7 +225,7 @@
             send(block, block, y2_send.at[j], y2_recv.at[j], at(dy=to % NY))
 
     def back_end(j):
-        wait(R2.at[j, pl.ds(0, NY - 3)], y2_recv.at[j])
+        wait(R2.at[j, pl.ds(0, NY - 1 if j in NEAR2 else NY - 3)], y2_recv.at[j])
         rows = pl.ds(CT * j, CT)
         full = []
         for a in range(3):
@@ -218,65 +247,64 @@
         n = (dot_nt(g0, Wg[0]) + dot_nt(g1, Wg[1]) + dot_nt(u0, Wu[0]) + dot_nt(u1, Wu[1])).reshape(NZ // 2, 8, D)
         even = jnp.where(low, m, pltpu.roll(n, TB, 1))
         odd = jnp.where(low, pltpu.roll(m, TB, 1), n)
-        for p in range(NZ // 2):
-            if j:
-                SX[j - 1, 2 * p] = coded2(even[p])
-                SX[j - 1, 2 * p + 1] = coded2(odd[p])
+        for b in range(NZ):
+            v = (odd if b % 2 else even)[b // 2]
+            g, dx = b // NX, b % NX
+            if dx:
+                SX[j, dx - 1, g] = coded2(v)
             else:
-                OX[2 * p] = even[p]
-                OX[2 * p + 1] = odd[p]
-        if j:
-            send(SX.at[j - 1], RX.at[NX - j - 1], rx_send.at[j - 1], rx_recv.at[NX - j - 1], at(dx=j))
-
-    f, b = FRONT, BACK
-    front(f[0])
-    front(f[1])
-    relay(f[0])
-    front(f[2])
-    relay(f[1])
-    front(f[3])
-    relay(f[2])
-    middle(b[0])
-    relay(f[3])
-    middle(b[1])
-    spread(b[0])
-    middle(b[2])
-    spread(b[1])
-    back_end(b[0])
-    middle(b[3])
-    spread(b[2])
-    back_end(b[1])
-    spread(b[3])
-    back_end(b[2])
-    back_end(b[3])
-
-    for i in range(2):
-        wait(T.at[1], t_recv.at[0]) if i == 0 else wait(G.at[1], t_recv.at[1])
-    for a in range(3):
-        wait(H.at[1, a], h_recv.at[a])
-    for a, (buf, out) in enumerate(((A1, ggate), (A2, gup))):
-        buf[...] = (dot_tn(T[0], H[0, a + 1]) + dot_tn(T[1], H[1, a + 1])).astype(BF16)
+                OX[j, g] = v
+        for dx in (2, 1, 3):
+            send(SX.at[j, dx - 1], RX.at[j, NX - dx - 1], rx_send.at[j], rx_recv.at[j], at(dx=dx))
+
+    def finish(j):
+        wait(RX.at[j], rx_recv.at[j])
+        own = None
+        for g in range(NG):
+            dz = Z_ORDER[NG * j + g]
+            v = OX[j, g] + jnp.sum(decoded2(RX[j, :, g]), axis=0)
+            if dz:
+                SZ[dz - 1] = coded2(v)
+                send(SZ.at[dz - 1], RZ.at[NZ - dz - 1], rz_send, rz_recv, at(dz=dz))
+            else:
+                OZ[...] = v
+
+    def turn(i):
+        if i == 0:
+            wait(T.at[1], t_recv.at[0])
+        half = D // 2
+        TT[half * i : half * (i + 1)] = T[:, :, half * i : half * (i + 1)].reshape(2 * NC * CT, half).T
+
+    def weight_grad(a):
+        b = (a + 1) % 3
+        wait(H.at[1, b], h_recv.at[b])
+        h = H[:, b].reshape(2 * NC * CT, F)
+        if a == 2:
+            wait(G.at[1], t_recv.at[1])
+            grad = dot_tn(h, G[...].reshape(2 * NC * CT, D))
+        else:
+            grad = dot(TT[...], h)
+        buf, out = ((A1, ggate), (A2, gup), (A3, gdown))[a]
+        buf[...] = grad.astype(BF16)
         pltpu.make_async_copy(buf, out, o_sem.at[a]).start()
 
-    for s in range(NX - 1):
-        wait(RX.at[s], rx_recv.at[s])
-    for dz in near[::-1]:
-        SZ[dz - 1] = coded2(OX[dz] + jnp.sum(decoded2(RX[:, dz]), axis=0))
-        send(SZ.at[dz - 1], RZ.at[NZ - dz - 1], rz_send, rz_recv, at(dz=dz))
-    total = OX[0] + jnp.sum(decoded2(RX[:, 0]), axis=0)
-
-    A3[...] = (dot_tn(H[0, 0], G[0]) + dot_tn(H[1, 0], G[1])).astype(BF16)
-    pltpu.make_async_copy(A3, gdown, o_sem.at[2]).start()
+    stages = dict(
+        pass_on=pass_on, front=front, relay=relay, middle=middle, spread=spread, back_end=back_end, finish=finish,
+        turn=turn, weight_grad=weight_grad,
+    )
+    for stage, *chunks in SCHEDULE:
+        for chunk in chunks:
+            stages[stage](chunk)
 
     wait(RZ, rz_recv)
-    total += jnp.sum(decoded2(RZ[...]), axis=0)
+    total = OZ[...] + jnp.sum(decoded2(RZ[...]), axis=0)
     tok[...] = total[:TB].astype(BF16)
     gout[...] = total[TB:].astype(BF16)
     pltpu.make_async_copy(tok, mixed, o_sem.at[3]).start()
     pltpu.make_async_copy(gout, gtok, o_sem.at[4]).start()
 
     wait(RZ, z_send)
-    wait(X.at[pl.ds(0, NX - 1)], x_send)
+    wait(X.at[pl.ds(0, NZ - NG)], x_send)
     wait(RZ, rz_send)
     for i, (src, dst) in enumerate(weights):
         wait(dst.at[0], wx_send.at[i])
@@ -284,8 +312,8 @@
     wait(G.at[0], t_send.at[1])
     for a in range(3):
         wait(HP.at[a], h_send.at[a])
-        wait(SX.at[a], rx_send.at[a])
-    for j in range(NX):
+    for j in range(NC):
+        wait(SX.at[j], rx_send.at[j])
         wait(R2.at[j, pl.ds(0, 7)], y1_send.at[j])
         wait(R2.at[j, pl.ds(0, 7)], y2_send.at[j])
     for a, (buf, out) in enumerate(((A1, ggate), (A2, gup), (A3, gdown), (tok, mixed), (gout, gtok))):
@@ -320,22 +348,24 @@
         scratch_shapes=[
             pltpu.VMEM((TB, D), BF16),
             pltpu.VMEM((TB, D), BF16),
-            pltpu.VMEM((NX, NZ, 8, D), BF16),
+            pltpu.VMEM((NZ, NX, 8, D), BF16),
             pltpu.VMEM((2, D, F), BF16),
             pltpu.VMEM((2, D, F), BF16),
             pltpu.VMEM((2, F, D), BF16),
-            pltpu.VMEM((2, NX * CT, D), BF16),
-            pltpu.VMEM((2, NX * CT, D), BF16),
-            pltpu.VMEM((NX, NY, 3, ROWS, LANES), BF16),
-            pltpu.VMEM((NX, 3, 3, ROWS, LANES), BF16),
-            pltpu.VMEM((NX, 2, 3, ROWS, LANES), BF16),
-            pltpu.VMEM((NX, 4, 3, ROWS, LANES), BF16),
-            pltpu.VMEM((NX, NY, 3, ROWS, LANES), BF16),
-            pltpu.VMEM((2, 3, NX * CT, F), BF16),
-            pltpu.VMEM((3, NX * CT, F), BF16),
-            pltpu.VMEM((NX - 1, NZ, 8, D), BF16),
-            pltpu.VMEM((NX - 1, NZ, 8, D), BF16),
-            pltpu.VMEM((NZ, 8, D), F32),
+            pltpu.VMEM((2, NC * CT, D), BF16),
+            pltpu.VMEM((2, NC * CT, D), BF16),
+            pltpu.VMEM((D, 2 * NC * CT), BF16),
+            pltpu.VMEM((NC, NY, 3, ROWS, LANES), BF16),
+            pltpu.VMEM((NC, 3, 3, ROWS, LANES), BF16),
+            pltpu.VMEM((NC, 2, 3, ROWS, LANES), BF16),
+            pltpu.VMEM((NC, NY - 1, 3, ROWS, LANES), BF16),
+            pltpu.VMEM((NC, NY, 3, ROWS, LANES), BF16),
+            pltpu.VMEM((2, 3, NC * CT, F), BF16),
+            pltpu.VMEM((3, NC * CT, F), BF16),
+            pltpu.VMEM((NC, NX - 1, NG, 8, D), BF16),
+            pltpu.VMEM((NC, NX - 1, NG, 8, D), BF16),
+            pltpu.VMEM((NC, NG, 8, D), F32),
+            pltpu.VMEM((8, D), F32),
             pltpu.VMEM((NZ - 1, 8, D), BF16),
             pltpu.VMEM((NZ - 1, 8, D), BF16),
             pltpu.VMEM((D, F), BF16),
@@ -348,7 +378,7 @@
             dma,
             dma((NZ - 1,)),
             dma,
-            dma((NX - 1,)),
+            dma((NC,)),
             dma((2,)),
             dma((2,)),
             dma((NX,)),
@@ -359,8 +389,8 @@
             dma((NX,)),
             dma((3,)),
             dma((3,)),
-            dma((3,)),
-            dma((3,)),
+            dma((NC,)),
+            dma((NC,)),
             dma,
             dma,
             dma((5,)),

time: 75.7 us -> 66.1 us (0.87)
  the two profiles are of different devices: /device:TPU:1 before, /device:TPU:16 now
where the time goes in v4:
time: 66.1 us; the launch traced here: 65.8 us
  Pallas kernels  65.2 us (99%)
    pallas_call x1, Pallas kernels, on_device(): pl.pallas_call(kernel, name='ffn', out_shape=out_shape, in_specs=[hbm, hb...  62.9 us
    pallas_call x1, Pallas kernels, on_device(): pl.pallas_call(store, name='store', out_shape=out_shape, in_specs=[hbm] *...  2.3 us

profile of v4, /device:TPU:16, one launch (start us, length us, event | category | flops | bytes accessed | tf_op | source)
XLA Modules:
  0.0 65.8 jit_solution(14624480192161623731)
XLA Ops:
  0.6 62.9 %ffn.1 = (bf16[4,1024]{1,0:T(4,128)(2,1)}, bf16[4,1024]{1,0:T(4,128)(2,1)}, bf16[1024,256]{1,0:T(8,128)(2,1)}, bf16[1024,256]{1,0:T(8,128)(2,1)}, bf16[256,1024]{1,0:T(8,128)(2,1)}) custom-call(bf16[4,1024]{1,0:T(4,128)(2,1)} %tok_in.1, bf16[4,1024]{1,0:T(4,128)(2,1)} %gout_in.1, bf16[1024,256]{1,0:T(8,128)(2,1)} %wg_in.1, bf16[1024,256]{1,0:T(8,128)(2,1)} %wu_in.1, ...), custom_call_target="tpu_custom_call" | custom-call | flops 1811939328 | bytes 8388608 | tf_op jit(solution)/shard_map/ffn/pallas_call | solution.py:342
  63.5 2.3 %store.1 = (bf16[4,1024]{1,0:T(4,128)(2,1)}, bf16[4,1024]{1,0:T(4,128)(2,1)}, bf16[1024,256]{1,0:T(8,128)(2,1)}, bf16[1024,256]{1,0:T(8,128)(2,1)}, bf16[256,1024]{1,0:T(8,128)(2,1)}) custom-call(bf16[4,1024]{1,0:T(4,128)(2,1)} %get-tuple-element.10.refs_0_, bf16[4,1024]{1,0:T(4,128)(2,1)} %get-tuple-element.11.refs_1_, ...), custom_call_target="tpu_custom_call" | custom-call | tf_op jit(solution)/shard_map/store/pallas_call | solution.py:405

commit v5 on v4

--- a/solution.py
+++ b/solution.py
@@ -24,13 +24,13 @@
 SCHEDULE = (
     ("pass_on", 0, 1, 2, 3),
     ("front", 0, 1, 2, 3),
-    ("relay", 0, 1, 2, 3),
+    ("relay", 1, 2, 3, 0),
     ("turn", 0),
-    ("middle", 0, 1, 2, 3),
+    ("middle", 1, 2, 3, 0),
     ("turn", 1),
-    ("spread", 0, 1, 2, 3),
-    ("back_end", 0, 1, 2, 3),
-    ("finish", 0, 1, 2, 3),
+    ("spread", 1, 2, 3, 0),
+    ("back_end", 1, 2, 3, 0),
+    ("finish", 1, 2, 3, 0),
     ("weight_grad", 0, 1, 2),
 )
 NEAR1 = ()
@@ -320,16 +320,28 @@
         pltpu.make_async_copy(buf, out, o_sem.at[a]).wait()
 
 
+PIECES = 4
+
+
 def store(*refs):
     n = (len(refs) - 2) // 3
-    src, dst, held, (read, write) = refs[:n], refs[n : 2 * n], refs[2 * n : 3 * n], refs[3 * n :]
+    read, write = refs[3 * n :]
+    parts = []
     for i in range(n):
-        pltpu.make_async_copy(src[i], held[i], read.at[i]).start()
-    for i in range(n):
-        pltpu.make_async_copy(src[i], held[i], read.at[i]).wait()
-        pltpu.make_async_copy(held[i], dst[i], write.at[i]).start()
-    for i in range(n):
-        pltpu.make_async_copy(held[i], dst[i], write.at[i]).wait()
+        rows = refs[i].shape[0]
+        step = rows // PIECES if rows > TB else rows
+        for k in range(rows // step):
+            part = pl.ds(k * step, step)
+            src, dst, held = (refs[i + m * n].at[part] for m in range(3))
+            a, b = read.at[i * PIECES + k], write.at[i * PIECES + k]
+            parts.append((pltpu.make_async_copy(src, held, a), pltpu.make_async_copy(held, dst, b)))
+    for load, _ in parts:
+        load.start()
+    for load, save in parts:
+        load.wait()
+        save.start()
+    for _, save in parts:
+        save.wait()
 
 
 def on_device(tokens, grad_out, gate_weight, up_weight, down_weight):
@@ -408,7 +420,7 @@
         out_shape=out_shape,
         in_specs=[hbm] * 5,
         out_specs=(hbm,) * 5,
-        scratch_shapes=[pltpu.VMEM(o.shape, o.dtype) for o in out_shape] + [dma((5,)), dma((5,))],
+        scratch_shapes=[pltpu.VMEM(o.shape, o.dtype) for o in out_shape] + [dma((5 * PIECES,)), dma((5 * PIECES,))],
         compiler_params=pltpu.CompilerParams(vmem_limit_bytes=62 * 2**20),
     )(*outs)
 

time: 66.1 us -> 65.7 us (level)
  no operation moved by 1% of the time
where the time goes in v5:
time: 65.7 us; the launch traced here: 65.5 us
  Pallas kernels  64.8 us (99%)
    pallas_call x1, Pallas kernels, on_device(): pl.pallas_call(kernel, name='ffn', out_shape=out_shape, in_specs=[hbm, hb...  62.3 us
    pallas_call x1, Pallas kernels, on_device(): pl.pallas_call(store, name='store', out_shape=out_shape, in_specs=[hbm] *...  2.5 us

profile of v5, /device:TPU:16, one launch (start us, length us, event | category | flops | bytes accessed | tf_op | source)
XLA Modules:
  0.0 65.5 jit_solution(18093583067592852645)
XLA Ops:
  0.6 62.3 %ffn.1 = (bf16[4,1024]{1,0:T(4,128)(2,1)}, bf16[4,1024]{1,0:T(4,128)(2,1)}, bf16[1024,256]{1,0:T(8,128)(2,1)}, bf16[1024,256]{1,0:T(8,128)(2,1)}, bf16[256,1024]{1,0:T(8,128)(2,1)}) custom-call(bf16[4,1024]{1,0:T(4,128)(2,1)} %tok_in.1, bf16[4,1024]{1,0:T(4,128)(2,1)} %gout_in.1, bf16[1024,256]{1,0:T(8,128)(2,1)} %wg_in.1, bf16[1024,256]{1,0:T(8,128)(2,1)} %wu_in.1, ...), custom_call_target="tpu_custom_call" | custom-call | flops 1811939328 | bytes 8388608 | tf_op jit(solution)/shard_map/ffn/pallas_call | solution.py:354
  63.0 2.5 %store.1 = (bf16[4,1024]{1,0:T(4,128)(2,1)}, bf16[4,1024]{1,0:T(4,128)(2,1)}, bf16[1024,256]{1,0:T(8,128)(2,1)}, bf16[1024,256]{1,0:T(8,128)(2,1)}, bf16[256,1024]{1,0:T(8,128)(2,1)}) custom-call(bf16[4,1024]{1,0:T(4,128)(2,1)} %get-tuple-element.10.refs_0_, bf16[4,1024]{1,0:T(4,128)(2,1)} %get-tuple-element.11.refs_1_, ...), custom_call_target="tpu_custom_call" | custom-call | tf_op jit(solution)/shard_map/store/pallas_call | solution.py:417

commit v6 on v4

--- a/solution.py
+++ b/solution.py
@@ -24,16 +24,16 @@
 SCHEDULE = (
     ("pass_on", 0, 1, 2, 3),
     ("front", 0, 1, 2, 3),
-    ("relay", 0, 1, 2, 3),
     ("turn", 0),
-    ("middle", 0, 1, 2, 3),
+    ("relay", 0),
+    ("middle", 1, 2, 3, 0),
     ("turn", 1),
-    ("spread", 0, 1, 2, 3),
-    ("back_end", 0, 1, 2, 3),
-    ("finish", 0, 1, 2, 3),
+    ("spread", 1, 2, 3, 0),
+    ("back_end", 1, 2, 3, 0),
+    ("finish", 1, 2, 3, 0),
     ("weight_grad", 0, 1, 2),
 )
-NEAR1 = ()
+NEAR1 = (1, 2, 3)
 NEAR2 = ()
 
 

time: 66.1 us -> 66 us (level)
  no operation moved by 1% of the time
where the time goes in v6:
time: 66 us; the launch traced here: 65.8 us
  Pallas kernels  65.1 us (99%)
    pallas_call x1, Pallas kernels, on_device(): pl.pallas_call(kernel, name='ffn', out_shape=out_shape, in_specs=[hbm, hb...  62.8 us
    pallas_call x1, Pallas kernels, on_device(): pl.pallas_call(store, name='store', out_shape=out_shape, in_specs=[hbm] *...  2.3 us

profile of v6, /device:TPU:16, one launch (start us, length us, event | category | flops | bytes accessed | tf_op | source)
XLA Modules:
  0.0 65.8 jit_solution(2657059888581856492)
XLA Ops:
  0.6 62.8 %ffn.1 = (bf16[4,1024]{1,0:T(4,128)(2,1)}, bf16[4,1024]{1,0:T(4,128)(2,1)}, bf16[1024,256]{1,0:T(8,128)(2,1)}, bf16[1024,256]{1,0:T(8,128)(2,1)}, bf16[256,1024]{1,0:T(8,128)(2,1)}) custom-call(bf16[4,1024]{1,0:T(4,128)(2,1)} %tok_in.1, bf16[4,1024]{1,0:T(4,128)(2,1)} %gout_in.1, bf16[1024,256]{1,0:T(8,128)(2,1)} %wg_in.1, bf16[1024,256]{1,0:T(8,128)(2,1)} %wu_in.1, ...), custom_call_target="tpu_custom_call" | custom-call | flops 1811939328 | bytes 8388608 | tf_op jit(solution)/shard_map/ffn/pallas_call | solution.py:342
  63.5 2.3 %store.1 = (bf16[4,1024]{1,0:T(4,128)(2,1)}, bf16[4,1024]{1,0:T(4,128)(2,1)}, bf16[1024,256]{1,0:T(8,128)(2,1)}, bf16[1024,256]{1,0:T(8,128)(2,1)}, bf16[256,1024]{1,0:T(8,128)(2,1)}) custom-call(bf16[4,1024]{1,0:T(4,128)(2,1)} %get-tuple-element.10.refs_0_, bf16[4,1024]{1,0:T(4,128)(2,1)} %get-tuple-element.11.refs_1_, ...), custom_call_target="tpu_custom_call" | custom-call | tf_op jit(solution)/shard_map/store/pallas_call | solution.py:405
